TPU v7x, 128 devices: a whole 4x4x4 slice. The times are simulated.
128 devices in a mesh: mrow: 4 (over x), mcol: 4 (over y), sub: 8 (over z, core).
Axes of the slice: x: 4, y: 4, z: 4, core: 2. Of those that a mesh axis runs over, the one named last changes fastest.
Arguments:
- deflation: bfloat16 [64, 64, 256, 1024], P(None, 'sub', 'mcol', 'mrow'), may hold values from -0.13258252 to 0.13258252
- reaction: float32 [64, 256, 1024], P('sub', 'mcol', 'mrow'), may hold values from 0.005 to 0.16
- vector_counts: int32 [128], P(('mrow', 'mcol', 'sub')), may hold values from 32 to 64
Outputs:
- coarse_factor: float32 [8192, 8192], P(('mrow', 'mcol', 'sub'))
All inputs are finite; a program needn't handle non-finite values.
Results may differ from a plain program's by a relative error of at most 0.0003.
Values may be sent and summed in bfloat16 or wider, within the bound.
A program may use at most 192 MiB of HBM per device.

v0:
```python
import functools

import jax
import jax.numpy as jnp
from jax import lax
from jax.experimental import pallas as pl
from jax.experimental.pallas import tpu as pltpu
from jax.sharding import PartitionSpec as P

MESH = pl.DeviceIdType.MESH
F32 = jnp.float32
BF16 = jnp.bfloat16
HI = lax.Precision.HIGHEST
K = 64
CX = 8
CY = 64
CZ = 256
ROWS = K * 8
SUB = 8
EARLY = 6


def dot_nt(a, b, precision=None):
    return lax.dot_general(
        a, b, (((1,), (1,)), ((), ())), precision=precision, preferred_element_type=F32
    )


def dot_nn(a, b, precision=None):
    return lax.dot_general(
        a, b, (((1,), (0,)), ((), ())), precision=precision, preferred_element_type=F32
    )


def dot_tn(a, b, precision=None):
    return lax.dot_general(
        a, b, (((0,), (0,)), ((), ())), precision=precision, preferred_element_type=F32
    )


def iota(shape, axis):
    return lax.broadcasted_iota(jnp.int32, shape, axis)


def fold(product):
    same = (iota(product.shape, 0) & 7) == (iota(product.shape, 1) & 7)
    kept = jnp.where(same, product, 0.0).reshape(K, 8, ROWS).sum(axis=1)
    collect = ((iota((ROWS, K), 0) >> 3) == iota((ROWS, K), 1)).astype(F32)
    return dot_nn(kept, collect, HI)


def assemble_kernel(
    defl,
    react,
    count,
    own_out,
    factor_out,
    product_out,
    mbuf,
    left,
    right,
    acc,
    weight,
    zrows,
    yedge,
    ylow,
    yhigh,
    yrecv,
    zrecv,
    xrecv_low,
    xrecv_high,
    mask_own,
    mask_recv,
    part_send,
    part_recv,
    chain,
    border,
    pivots,
    solver,
    xin,
    xall,
    load_sem,
    mask_send_sem,
    mask_recv_sem,
    face_send_sem,
    face_recv_sem,
    y_send_sem,
    y_recv_sem,
    z_send_sem,
    z_recv_sem,
    part_send_sem,
    part_recv_sem,
    chain_send_sem,
    chain_recv_sem,
    border_send_sem,
    border_recv_sem,
    cross_send_sem,
    solver_send_sem,
    solver_recv_sem,
):
    mrow = lax.axis_index("mrow")
    mcol = lax.axis_index("mcol")
    sub = lax.axis_index("sub")
    mrows = lax.axis_size("mrow")
    mcols = lax.axis_size("mcol")
    s_next, s_prev = lax.rem(sub + 1, SUB), lax.rem(sub + SUB - 1, SUB)
    j_next, j_prev = lax.rem(mcol + 1, mcols), lax.rem(mcol + mcols - 1, mcols)
    i_next, i_prev = lax.rem(mrow + 1, mrows), lax.rem(mrow + mrows - 1, mrows)
    head = (mrow == 0) & (mcol == 0)
    second = (mrow == 0) & (mcol == 1)
    third = (mrow == 1) & (mcol == 0)

    loads = [
        pltpu.make_async_copy(defl.at[:, x], mbuf.at[x], load_sem.at[x]) for x in range(CX)
    ]
    for load in loads:
        load.start()

    barrier = pltpu.get_barrier_semaphore()
    for step in range(1, SUB):
        pl.semaphore_signal(
            barrier,
            inc=1,
            device_id={"sub": lax.rem(sub + step, SUB)},
            device_id_type=MESH,
        )
    for axis, other in (
        ("mcol", j_next),
        ("mcol", j_prev),
        ("mrow", i_next),
        ("mrow", i_prev),
    ):
        pl.semaphore_signal(barrier, inc=1, device_id={axis: other}, device_id_type=MESH)

    live = count[0]
    mask_own[...] = (iota((8, 128), 1) < live).astype(F32)
    weight[...] = 3.0 + 0.5 * react[...]
    mbuf[CX] = jnp.zeros((K, CY, CZ), BF16)
    acc[...] = jnp.zeros_like(acc)
    part_send[...] = jnp.zeros_like(part_send)
    tail = iota((16, 8 * CZ), 0)
    spot = (tail & 7) * CZ + (tail >> 3) * (CZ - 1)
    left[ROWS : ROWS + 16, :] = (iota((16, 8 * CZ), 1) == spot).astype(F32).astype(BF16)

    pl.semaphore_wait(barrier, SUB - 1 + 4)

    def remote(src, dst, send, recv, target):
        return pltpu.make_async_remote_copy(
            src_ref=src,
            dst_ref=dst,
            send_sem=send,
            recv_sem=recv,
            device_id=target,
            device_id_type=MESH,
        )

    xface_up = remote(
        defl.at[:, CX - 1, 0 : CY // 2],
        xrecv_low,
        face_send_sem.at[0],
        face_recv_sem.at[0],
        {"sub": s_next},
    )
    xface_down = remote(
        defl.at[:, 0, CY // 2 : CY],
        xrecv_high,
        face_send_sem.at[1],
        face_recv_sem.at[1],
        {"sub": s_prev},
    )
    xface_up.start()
    xface_down.start()

    masks = []
    for slot, target in enumerate(
        (
            {"sub": s_next},
            {"sub": s_prev},
            {"mcol": j_next},
            {"mcol": j_prev},
            {"mrow": i_next},
            {"mrow": i_prev},
        )
    ):
        masks.append(
            remote(
                mask_own,
                mask_recv.at[slot],
                mask_send_sem.at[slot],
                mask_recv_sem.at[slot],
                target,
            )
        )
        masks[-1].start()

    group = 4
    last_lane = iota((1, 1, 128), 2) == 127
    last_row = iota((1, 8, 1), 1) == 7

    def flat(value):
        return value.reshape(8 * group, CZ).astype(BF16)

    def stage_group(x, first, row):
        here = mbuf[x, pl.ds(first, group)].astype(F32)
        after_x = mbuf[x + 1, pl.ds(first, group)].astype(F32)
        turned_low = pltpu.roll(here[:, :, 0:128], 127, 2)
        turned_high = pltpu.roll(here[:, :, 128:256], 127, 2)
        after_z = jnp.concatenate(
            [
                jnp.where(last_lane, turned_high, turned_low),
                jnp.where(last_lane, 0.0, turned_high),
            ],
            axis=2,
        )
        turned = [pltpu.roll(here[:, 8 * n : 8 * n + 8, :], 7, 1) for n in range(8)]
        turned.append(jnp.zeros((group, 8, CZ), F32))
        place = pl.ds(row, 8 * group)
        for block in range(8):
            part = slice(8 * block, 8 * block + 8)
            lanes = slice(block * CZ, (block + 1) * CZ)
            after_y = jnp.where(last_row, turned[block + 1], turned[block])
            half = weight[x, part][None] * here[:, part] - after_x[:, part]
            half = half - after_y - after_z[:, part]
            left[place, lanes] = flat(half)
            right[place, lanes] = flat(here[:, part])
        for n in range(group):
            yedge[0, pl.ds(first + n, 1), :] = here[n, 0:1, :]
            yedge[1, pl.ds(first + n, 1), :] = here[n, CY - 1 : CY, :]

    def y_face(x):
        return remote(
            yhigh.at[x], yrecv.at[x], y_send_sem.at[x], y_recv_sem.at[x], {"mcol": j_next}
        )

    def z_face(x):
        return remote(
            zrows.at[x, pl.ds(8, 8)],
            zrecv.at[x],
            z_send_sem.at[x],
            z_recv_sem.at[x],
            {"mrow": i_next},
        )

    def plane(x, carry):
        @pl.when(x < EARLY)
        def _():
            pltpu.make_async_copy(
                defl.at[:, x + 1], mbuf.at[x + 1], load_sem.at[x + 1]
            ).wait()

        def part(step, inner):
            for q in range(K // 2 // group):
                first = pl.multiple_of(step * (K // 2) + q * group, group)
                row = pl.multiple_of(step * (K // 2 * 8) + q * group * 8, group * 8)
                stage_group(x, first, row)
            return inner

        lax.fori_loop(0, 2, part, 0)
        ylow[x] = yedge[0].astype(BF16)
        yhigh[x] = yedge[1].astype(BF16)
        y_face(x).start()
        product = dot_nt(left[...], right[...])
        acc[...] += product[:ROWS]
        zrows[x] = product[ROWS : ROWS + 16]
        z_face(x).start()
        return carry

    loads[0].wait()
    lax.fori_loop(0, EARLY, plane, 0)

    for load in loads[EARLY + 1 :]:
        load.wait()
    xface_up.wait()
    xface_down.wait()

    def stage(step, inner):
        for q in range(2):
            first = pl.multiple_of(8 * step + q * group, group)
            place = pl.ds(pl.multiple_of(64 * step + q * group * 8, group * 8), group * 8)
            chosen = pl.ds(first, group)
            sources = (
                (mbuf[0, chosen, 0 : CY // 2, :], xrecv_low[chosen]),
                (last_half[chosen], xrecv_high[chosen]),
            )
            for which, (mine, theirs) in enumerate(sources):
                mine = mine.astype(F32)
                theirs = theirs.astype(F32)
                for block in range(4):
                    part = slice(8 * block, 8 * block + 8)
                    lanes = slice((4 * which + block) * CZ, (4 * which + block + 1) * CZ)
                    right[place, lanes] = flat(mine[:, part])
                    left[place, lanes] = flat(theirs[:, part])
        return inner

    last_half = mbuf.at[CX - 1, :, CY // 2 : CY, :]
    lax.fori_loop(0, K // 8, stage, 0)
    low_part = fold(dot_nt(left[0:ROWS, 0 : 4 * CZ], right[:, 0 : 4 * CZ]))
    high_part = fold(dot_nt(right[:, 4 * CZ : 8 * CZ], left[0:ROWS, 4 * CZ : 8 * CZ]))
    part_send[0, :, 0:K] = low_part
    part_send[1, :, 0:K] = high_part.T
    parts = [
        remote(
            part_send.at[slot],
            part_recv.at[slot],
            part_send_sem.at[slot],
            part_recv_sem.at[slot],
            target,
        )
        for slot, target in enumerate(
            ({"sub": s_prev}, {"sub": s_next}, {"mcol": j_prev}, {"mrow": i_prev})
        )
    ]
    parts[0].start()
    parts[1].start()

    lax.fori_loop(EARLY, CX, plane, 0)

    own_row = (iota((K, K), 0) < live).astype(F32)
    own_col = mask_own[0:1, 0:K]
    diag = (iota((K, K), 0) == iota((K, K), 1)).astype(F32)

    def finish(block, slot, present):
        kept = own_row * mask_recv[slot, 0:1, 0:K]
        return -block * (kept * jnp.where(present, 1.0, 0.0))

    gram = fold(acc[...])
    diagonal = (gram + gram.T) * own_row * own_col + diag * (1.0 - own_row)
    for mask in masks:
        mask.wait()
    parts[0].wait()
    parts[1].wait()
    x_low = finish(low_part.T + part_recv[1, :, 0:K], 0, sub > 0)
    x_high = finish(high_part + part_recv[0, :, 0:K], 1, sub < SUB - 1)
    own_out[:, 0 : 2 * K] = jnp.concatenate([diagonal, x_high], axis=1)

    def cross(buffer, recv, which):
        return remote(
            buffer.at[sub],
            buffer.at[sub],
            cross_send_sem.at[which],
            recv.at[sub],
            ({"mcol": j_next}, {"mrow": i_next})[which],
        )

    def line(buffer, send, recv, step):
        return remote(
            buffer.at[sub],
            buffer.at[sub],
            send.at[step],
            recv.at[sub],
            {"sub": lax.rem(sub + step, SUB)},
        )

    def landed(buffer, recv, slot):
        return remote(
            buffer.at[slot],
            buffer.at[slot],
            cross_send_sem.at[0],
            recv.at[slot],
            {"mcol": j_next},
        )

    @pl.when(head)
    def _():
        chain[sub] = jnp.concatenate([diagonal, x_high], axis=1)
        for step in range(1, SUB):
            line(chain, chain_send_sem, chain_recv_sem, step).start()

    for x in range(CX):
        y_face(x).wait()
        z_face(x).wait()
    y_part = dot_nt(
        jnp.concatenate([yrecv[x] for x in range(CX)], axis=1),
        jnp.concatenate([ylow[x] for x in range(CX)], axis=1),
    )
    part_send[2, :, 0:K] = y_part
    parts[2].start()
    z_low = zrows[:, 0:8, :].reshape(K, ROWS)
    z_part = fold(dot_tn(zrecv[...].reshape(K, ROWS), z_low))
    part_send[3, :, 0:K] = z_part
    parts[3].start()
    y_low = finish(y_part.T, 2, mcol > 0)
    z_lower = finish(z_part.T, 4, mrow > 0)

    def start_border():
        parts[2].wait()
        parts[3].wait()
        y_high = finish(part_recv[2, :, 0:K], 3, mcol < mcols - 1)
        z_high = finish(part_recv[3, :, 0:K], 5, mrow < mrows - 1)
        own_out[:, 2 * K : 8 * K] = jnp.concatenate(
            [y_high, z_high, x_low, y_low, z_lower, jnp.zeros((K, K), F32)], axis=1
        )

        @pl.when(head)
        def _():
            border[sub] = jnp.concatenate([y_high, z_high], axis=1)
            cross(border, border_recv_sem, 0).start()
            cross(border, border_recv_sem, 1).start()

    def eliminate(index, pivot):
        coupling = chain[index][:, K : 2 * K]
        unit = (iota((K, K), 0) == iota((K, K), 1)).astype(F32)
        state = jnp.concatenate([pivot, jnp.zeros((K, K), F32)], axis=1)
        extra = jnp.concatenate([coupling, unit], axis=1)
        state = [state[8 * n : 8 * n + 8] for n in range(8)]
        inverse = [extra[8 * n : 8 * n + 8] for n in range(8)]
        for now in range(8):
            columns = {
                n: [
                    jnp.broadcast_to(state[n][:, 8 * now + c : 8 * now + c + 1], (8, 128))
                    for c in range(8)
                ]
                for n in range(now, 8)
            }
            lower = {}
            scale = []
            for c in range(8):
                value = columns[now][c][c : c + 1]
                for k in range(c):
                    value = value - lower[c, k] * lower[c, k]
                scale.append(lax.rsqrt(value))
                for r in range(c + 1, 8):
                    value = columns[now][c][r : r + 1]
                    for k in range(c):
                        value = value - lower[r, k] * lower[c, k]
                    lower[r, c] = value * scale[c]
            lines, lines_inverse = [], []
            for c in range(8):
                line_now = state[now][c : c + 1]
                line_inverse = inverse[now][c : c + 1]
                for k in range(c):
                    line_now = line_now - lower[c, k] * lines[k]
                    line_inverse = line_inverse - lower[c, k] * lines_inverse[k]
                lines.append(line_now * scale[c])
                lines_inverse.append(line_inverse * scale[c])
                at = 8 * now + c
                pivots[index, at : at + 1, :] = lines[c]
                solver[index, at : at + 1, :] = lines_inverse[c]
            for n in range(now + 1, 8):
                factors = []
                for c in range(8):
                    factor = columns[n][c]
                    for k in range(c):
                        factor = factor - factors[k] * lower[c, k]
                    factors.append(factor * scale[c])
                for c in range(8):
                    state[n] = state[n] - factors[c] * lines[c]
                    inverse[n] = inverse[n] - factors[c] * lines_inverse[c]

    def arrive(buffer, recv, slot):
        @pl.when(sub != slot)
        def _():
            landed(buffer, recv, slot).wait_recv()

    def result(index, which):
        return remote(
            solver.at[index],
            solver.at[index],
            solver_send_sem.at[index, which],
            solver_recv_sem.at[index],
            ({"mcol": j_next}, {"mrow": i_next})[which],
        )

    def factor(index, pivot):
        following = jnp.minimum(index + 1, SUB - 1)

        @pl.when(index < SUB - 1)
        def _():
            arrive(chain, chain_recv_sem, following)

        eliminate(index, pivot)
        result(index, 0).start()
        result(index, 1).start()
        coupled = solver[index, :, 0:K]
        return chain[following][:, 0:K] - dot_tn(coupled, coupled, HI)

    lane = iota((K, 8 * K), 1) >> 6

    def placed(index):
        values = border[index]
        first = jnp.concatenate([values[:, 0:K]] * 8, axis=1)
        other = jnp.concatenate([values[:, K : 2 * K]] * 8, axis=1)
        first = jnp.where(lane == index, first, 0.0)
        other = jnp.where(lane == index, other, 0.0)
        return jnp.concatenate([first, other], axis=1)

    def solve(index, carry):
        result(index, 0).wait_recv()
        values = solver[index]
        solved = dot_nn(values[:, K : 2 * K], xin[...], HI)
        xall[pl.ds(pl.multiple_of(index * K, K), K), :] = solved
        following = placed(jnp.minimum(index + 1, SUB - 1))
        xin[...] = following - dot_tn(values[:, 0:K], solved, HI)
        return carry

    @pl.when(head)
    def _():
        arrive(chain, chain_recv_sem, 0)
        pivot = lax.fori_loop(0, 1, factor, chain[0][:, 0:K])
        start_border()
        lax.fori_loop(1, SUB, factor, pivot)

    @pl.when(jnp.logical_not(head))
    def _():
        start_border()

    @pl.when(head)
    def _():
        upper = iota((K, K), 0) <= iota((K, K), 1)
        factor_out[:, 0:K] = jnp.where(upper, pivots[sub, :, 0:K], 0.0).T
        factor_out[:, K : 2 * K] = solver[jnp.maximum(sub - 1, 0), :, 0:K].T
        for step in range(1, SUB):
            line(chain, chain_send_sem, chain_recv_sem, step).wait_send()
        for which in range(2):
            cross(border, border_recv_sem, which).wait_send()
            for index in range(SUB):
                result(index, which).wait_send()

    @pl.when(second | third)
    def _():
        landed(border, border_recv_sem, sub).wait_recv()
        for step in range(1, SUB):
            line(border, border_send_sem, border_recv_sem, step).start()
        for slot in range(SUB):
            arrive(border, border_recv_sem, slot)
        xin[...] = placed(0)
        lax.fori_loop(0, SUB, solve, 0)
        which = jnp.where(third, SUB, 0) + sub
        mine = xall[:, pl.ds(pl.multiple_of((which // 2) * 128, 128), 128)]
        mine = jnp.where(lax.rem(sub, 2) == 1, pltpu.roll(mine, K, 1), mine)
        factor_out[...] = mine.T[0:K, :]
        product_out[...] = dot_tn(mine, xall[...], HI)[0:K]
        for step in range(1, SUB):
            line(border, border_send_sem, border_recv_sem, step).wait_send()


def place_kernel(own_hbm, factors_hbm, product_hbm, out, own, factors, product, sems):
    copies = [
        pltpu.make_async_copy(source, target, sems.at[n])
        for n, (source, target) in enumerate(
            ((own_hbm, own), (factors_hbm, factors), (product_hbm, product))
        )
    ]
    for copy in copies:
        copy.start()
    mrow = lax.axis_index("mrow")
    mcol = lax.axis_index("mcol")
    sub = lax.axis_index("sub")
    mrows = lax.axis_size("mrow")
    mcols = lax.axis_size("mcol")
    position = (mrow * mcols + mcol) * SUB + sub
    head = (mrow == 0) & (mcol == 0)
    second = (mrow == 0) & (mcol == 1)
    third = (mrow == 1) & (mcol == 0)
    odd = lax.rem(sub, 2) == 1

    out[...] = jnp.zeros_like(out)
    for copy in copies:
        copy.wait()

    def tile(index):
        return pl.ds(pl.multiple_of(index * 128, 128), 128)

    def block(index):
        return own[:, index * K : (index + 1) * K]

    empty = jnp.zeros((K, K), F32)

    @pl.when(jnp.logical_not(head))
    def _():
        diagonal, x_high, y_high, z_high, x_low, y_low, z_low = (block(n) for n in range(7))
        here = position // 2
        pair_even = jnp.concatenate([diagonal, x_high], axis=1)
        pair_odd = jnp.concatenate([x_low, diagonal], axis=1)
        out[:, tile(here)] = jnp.where(odd, pair_odd, pair_even)

        @pl.when(odd & (sub < SUB - 1))
        def _():
            out[:, tile(here + 1)] = jnp.concatenate([x_high, empty], axis=1)

        @pl.when(jnp.logical_not(odd) & (sub > 0))
        def _():
            out[:, tile(here - 1)] = jnp.concatenate([empty, x_low], axis=1)

        def either(value):
            return jnp.where(
                odd,
                jnp.concatenate([empty, value], axis=1),
                jnp.concatenate([value, empty], axis=1),
            )

        for value, present, stride in (
            (y_high, mcol < mcols - 1, SUB // 2),
            (y_low, (mcol > 0) & jnp.logical_not(second), -(SUB // 2)),
            (z_high, mrow < mrows - 1, mcols * SUB // 2),
            (z_low, (mrow > 0) & jnp.logical_not(third), -(mcols * SUB // 2)),
        ):

            @pl.when(present)
            def _():
                out[:, tile(here + stride)] = either(value)

    @pl.when(head)
    def _():
        mine = factors[:, 0:K]
        before = factors[:, K : 2 * K]
        here = sub // 2
        out[:, tile(here)] = jnp.where(
            odd,
            jnp.concatenate([before, mine], axis=1),
            jnp.concatenate([mine, empty], axis=1),
        )

        @pl.when(jnp.logical_not(odd) & (sub > 0))
        def _():
            out[:, tile(here - 1)] = jnp.concatenate([empty, before], axis=1)

    @pl.when(second | third)
    def _():
        out[:, 0 : 8 * K] = factors[...]
        out[:, 8 * K : 16 * K] -= product[:, 0 : 8 * K]
        far = mcols * SUB * K
        out[:, far : far + 8 * K] -= product[:, 8 * K : 16 * K]


def shards(deflation, reaction, vector_counts):
    vmem = pl.BlockSpec(memory_space=pltpu.VMEM)
    results = pl.pallas_call(
        assemble_kernel,
        out_shape=(
            jax.ShapeDtypeStruct((K, 8 * K), F32),
            jax.ShapeDtypeStruct((K, 8 * K), F32),
            jax.ShapeDtypeStruct((K, 16 * K), F32),
        ),
        in_specs=[
            pl.BlockSpec(memory_space=pl.ANY),
            vmem,
            pl.BlockSpec(memory_space=pltpu.SMEM),
        ],
        out_specs=(vmem, vmem, vmem),
        scratch_shapes=[
            pltpu.VMEM((CX + 1, K, CY, CZ), BF16),
            pltpu.VMEM((ROWS + 16, 8 * CZ), BF16),
            pltpu.VMEM((ROWS, 8 * CZ), BF16),
            pltpu.VMEM((ROWS, ROWS), F32),
            pltpu.VMEM((CX, CY, CZ), F32),
            pltpu.VMEM((CX, 16, ROWS), F32),
            pltpu.VMEM((2, K, CZ), F32),
            pltpu.VMEM((CX, K, CZ), BF16),
            pltpu.VMEM((CX, K, CZ), BF16),
            pltpu.VMEM((CX, K, CZ), BF16),
            pltpu.VMEM((CX, 8, ROWS), F32),
            pltpu.VMEM((K, CY // 2, CZ), BF16),
            pltpu.VMEM((K, CY // 2, CZ), BF16),
            pltpu.VMEM((8, 128), F32),
            pltpu.VMEM((6, 8, 128), F32),
            pltpu.VMEM((4, K, 128), F32),
            pltpu.VMEM((4, K, 128), F32),
            pltpu.VMEM((SUB, K, 2 * K), F32),
            pltpu.VMEM((SUB, K, 2 * K), F32),
            pltpu.VMEM((SUB, K, 128), F32),
            pltpu.VMEM((SUB, K, 2 * K), F32),
            pltpu.VMEM((K, 16 * K), F32),
            pltpu.VMEM((SUB * K, 16 * K), F32),
            pltpu.SemaphoreType.DMA((CX,)),
            pltpu.SemaphoreType.DMA((6,)),
            pltpu.SemaphoreType.DMA((6,)),
            pltpu.SemaphoreType.DMA((2,)),
            pltpu.SemaphoreType.DMA((2,)),
            pltpu.SemaphoreType.DMA((CX,)),
            pltpu.SemaphoreType.DMA((CX,)),
            pltpu.SemaphoreType.DMA((CX,)),
            pltpu.SemaphoreType.DMA((CX,)),
            pltpu.SemaphoreType.DMA((4,)),
            pltpu.SemaphoreType.DMA((4,)),
            pltpu.SemaphoreType.DMA((SUB,)),
            pltpu.SemaphoreType.DMA((SUB,)),
            pltpu.SemaphoreType.DMA((SUB,)),
            pltpu.SemaphoreType.DMA((SUB,)),
            pltpu.SemaphoreType.DMA((2,)),
            pltpu.SemaphoreType.DMA((SUB, 2)),
            pltpu.SemaphoreType.DMA((SUB,)),
        ],
        compiler_params=pltpu.CompilerParams(
            collective_id=0, has_side_effects=True, vmem_limit_bytes=56 * 1024 * 1024
        ),
        name="assemble",
    )(deflation, reaction, vector_counts)
    return pl.pallas_call(
        place_kernel,
        out_shape=jax.ShapeDtypeStruct((K, 128 * K), F32),
        in_specs=[pl.BlockSpec(memory_space=pl.ANY)] * 3,
        out_specs=vmem,
        scratch_shapes=[
            pltpu.VMEM((K, 8 * K), F32),
            pltpu.VMEM((K, 8 * K), F32),
            pltpu.VMEM((K, 16 * K), F32),
            pltpu.SemaphoreType.DMA((3,)),
        ],
        compiler_params=pltpu.CompilerParams(vmem_limit_bytes=56 * 1024 * 1024),
        name="place",
    )(*results)


def solution(mesh):
    return jax.shard_map(
        shards,
        mesh=mesh,
        in_specs=(
            P(None, "sub", "mcol", "mrow"),
            P("sub", "mcol", "mrow"),
            P(("mrow", "mcol", "sub")),
        ),
        out_specs=P(("mrow", "mcol", "sub"), None),
        check_vma=False,
    )
```

profile of v0, /device:TPU:2, one launch (start us, length us, event | category | flops | bytes accessed | tf_op | source)
XLA Modules:
  0.0 62.6 jit_solution(6227443395541723184)
XLA Ops:
  0.7 59.3 %assemble.1 = (f32[64,512]{1,0:T(8,128)}, f32[64,512]{1,0:T(8,128)}, f32[64,1024]{1,0:T(8,128)}) custom-call(bf16[64,8,64,256]{3,2,1,0:T(8,128)(2,1)} %defl.1, f32[8,64,256]{2,1,0:T(8,128)} %react.1, s32[1]{0:T(128)S(6)} %copy.4.count), custom_call_target="tpu_custom_call" | custom-call | tf_op jit(solution)/shard_map/assemble/pallas_call | solution.py:628
  60.0 2.7 %place.1 = f32[64,8192]{1,0:T(8,128)} custom-call(f32[64,512]{1,0:T(8,128)} %get-tuple-element.8.own_hbm, f32[64,512]{1,0:T(8,128)} %get-tuple-element.9.factors_hbm, f32[64,1024]{1,0:T(8,128)} %get-tuple-element.10.product_hbm), custom_call_target="tpu_custom_call" | custom-call | tf_op jit(solution)/shard_map/place/pallas_call | solution.py:689
where the time goes:
time: 62.8 us; the launch traced here: 62.6 us
  Pallas kernels  62 us (99%)
  between operations  0.66 us (1%)
    pallas_call x1, Pallas kernels, shards(): pl.pallas_call(assemble_kernel, out_shape=(jax.ShapeDtypeStruct((K, 8 * K...  59.3 us
    pallas_call x1, Pallas kernels, shards(): pl.pallas_call(place_kernel, out_shape=jax.ShapeDtypeStruct((K, 128 * K),...  2.69 us

commit v1 on v0

--- a/solution.py
+++ b/solution.py
@@ -36,6 +36,17 @@
     return lax.dot_general(
         a, b, (((0,), (0,)), ((), ())), precision=precision, preferred_element_type=F32
     )
+
+
+def halves(value):
+    high = value.astype(BF16)
+    return high, (value - high.astype(F32)).astype(BF16)
+
+
+def triple(dot, a, b):
+    a_high, a_low = halves(a)
+    b_high, b_low = halves(b)
+    return dot(a_high, b_high) + (dot(a_high, b_low) + dot(a_low, b_high))
 
 
 def iota(shape, axis):
@@ -77,6 +88,7 @@
     border,
     pivots,
     solver,
+    spread,
     xin,
     xall,
     load_sem,
@@ -142,8 +154,6 @@
     spot = (tail & 7) * CZ + (tail >> 3) * (CZ - 1)
     left[ROWS : ROWS + 16, :] = (iota((16, 8 * CZ), 1) == spot).astype(F32).astype(BF16)
 
-    pl.semaphore_wait(barrier, SUB - 1 + 4)
-
     def remote(src, dst, send, recv, target):
         return pltpu.make_async_remote_copy(
             src_ref=src,
@@ -168,31 +178,6 @@
         face_recv_sem.at[1],
         {"sub": s_prev},
     )
-    xface_up.start()
-    xface_down.start()
-
-    masks = []
-    for slot, target in enumerate(
-        (
-            {"sub": s_next},
-            {"sub": s_prev},
-            {"mcol": j_next},
-            {"mcol": j_prev},
-            {"mrow": i_next},
-            {"mrow": i_prev},
-        )
-    ):
-        masks.append(
-            remote(
-                mask_own,
-                mask_recv.at[slot],
-                mask_send_sem.at[slot],
-                mask_recv_sem.at[slot],
-                target,
-            )
-        )
-        masks[-1].start()
-
     group = 4
     last_lane = iota((1, 1, 128), 2) == 127
     last_row = iota((1, 8, 1), 1) == 7
@@ -241,7 +226,19 @@
             {"mrow": i_next},
         )
 
-    def plane(x, carry):
+    y_up, y_down = mcol < mcols - 1, mcol > 0
+    z_up, z_down = mrow < mrows - 1, mrow > 0
+
+    def start_faces(x):
+        @pl.when(y_up)
+        def _():
+            y_face(x).start()
+
+        @pl.when(z_up)
+        def _():
+            z_face(x).start()
+
+    def silent_plane(x, carry):
         @pl.when(x < EARLY)
         def _():
             pltpu.make_async_copy(
@@ -258,15 +255,45 @@
         lax.fori_loop(0, 2, part, 0)
         ylow[x] = yedge[0].astype(BF16)
         yhigh[x] = yedge[1].astype(BF16)
-        y_face(x).start()
         product = dot_nt(left[...], right[...])
         acc[...] += product[:ROWS]
         zrows[x] = product[ROWS : ROWS + 16]
-        z_face(x).start()
         return carry
 
+    def plane(x, carry):
+        silent_plane(x, carry)
+        start_faces(x)
+        return carry
+
     loads[0].wait()
-    lax.fori_loop(0, EARLY, plane, 0)
+    lax.fori_loop(0, 1, silent_plane, 0)
+    pl.semaphore_wait(barrier, SUB - 1 + 4)
+    xface_up.start()
+    xface_down.start()
+
+    masks = []
+    for slot, target in enumerate(
+        (
+            {"sub": s_next},
+            {"sub": s_prev},
+            {"mcol": j_next},
+            {"mcol": j_prev},
+            {"mrow": i_next},
+            {"mrow": i_prev},
+        )
+    ):
+        masks.append(
+            remote(
+                mask_own,
+                mask_recv.at[slot],
+                mask_send_sem.at[slot],
+                mask_recv_sem.at[slot],
+                target,
+            )
+        )
+        masks[-1].start()
+    start_faces(0)
+    lax.fori_loop(1, EARLY, plane, 0)
 
     for load in loads[EARLY + 1 :]:
         load.wait()
@@ -329,9 +356,7 @@
         mask.wait()
     parts[0].wait()
     parts[1].wait()
-    x_low = finish(low_part.T + part_recv[1, :, 0:K], 0, sub > 0)
     x_high = finish(high_part + part_recv[0, :, 0:K], 1, sub < SUB - 1)
-    own_out[:, 0 : 2 * K] = jnp.concatenate([diagonal, x_high], axis=1)
 
     def cross(buffer, recv, which):
         return remote(
@@ -366,30 +391,51 @@
         for step in range(1, SUB):
             line(chain, chain_send_sem, chain_recv_sem, step).start()
 
-    for x in range(CX):
-        y_face(x).wait()
-        z_face(x).wait()
-    y_part = dot_nt(
-        jnp.concatenate([yrecv[x] for x in range(CX)], axis=1),
-        jnp.concatenate([ylow[x] for x in range(CX)], axis=1),
-    )
-    part_send[2, :, 0:K] = y_part
-    parts[2].start()
-    z_low = zrows[:, 0:8, :].reshape(K, ROWS)
-    z_part = fold(dot_tn(zrecv[...].reshape(K, ROWS), z_low))
-    part_send[3, :, 0:K] = z_part
-    parts[3].start()
-    y_low = finish(y_part.T, 2, mcol > 0)
-    z_lower = finish(z_part.T, 4, mrow > 0)
+    x_low = finish(low_part.T + part_recv[1, :, 0:K], 0, sub > 0)
+    own_out[:, 0 : 2 * K] = jnp.concatenate([diagonal, x_high], axis=1)
+    own_out[:, 4 * K : 5 * K] = x_low
+
+    @pl.when(y_down)
+    def _():
+        for x in range(CX):
+            y_face(x).wait_recv()
+        y_part = dot_nt(
+            jnp.concatenate([yrecv[x] for x in range(CX)], axis=1),
+            jnp.concatenate([ylow[x] for x in range(CX)], axis=1),
+        )
+        part_send[2, :, 0:K] = y_part
+        parts[2].start()
+        own_out[:, 5 * K : 6 * K] = finish(y_part.T, 2, True)
+
+    @pl.when(z_down)
+    def _():
+        for x in range(CX):
+            z_face(x).wait_recv()
+        z_low = zrows[:, 0:8, :].reshape(K, ROWS)
+        z_part = fold(dot_tn(zrecv[...].reshape(K, ROWS), z_low))
+        part_send[3, :, 0:K] = z_part
+        parts[3].start()
+        own_out[:, 6 * K : 7 * K] = finish(z_part.T, 4, True)
 
     def start_border():
-        parts[2].wait()
-        parts[3].wait()
-        y_high = finish(part_recv[2, :, 0:K], 3, mcol < mcols - 1)
-        z_high = finish(part_recv[3, :, 0:K], 5, mrow < mrows - 1)
-        own_out[:, 2 * K : 8 * K] = jnp.concatenate(
-            [y_high, z_high, x_low, y_low, z_lower, jnp.zeros((K, K), F32)], axis=1
-        )
+        for up, down, part, face in (
+            (y_up, y_down, parts[2], y_face),
+            (z_up, z_down, parts[3], z_face),
+        ):
+
+            @pl.when(up)
+            def _():
+                part.wait_recv()
+                for x in range(CX):
+                    face(x).wait_send()
+
+            @pl.when(down)
+            def _():
+                part.wait_send()
+
+        y_high = finish(part_recv[2, :, 0:K], 3, y_up)
+        z_high = finish(part_recv[3, :, 0:K], 5, z_up)
+        own_out[:, 2 * K : 4 * K] = jnp.concatenate([y_high, z_high], axis=1)
 
         @pl.when(head)
         def _():
@@ -412,15 +458,21 @@
                 ]
                 for n in range(now, 8)
             }
+            for c in range(8):
+                spread[now % 2, c] = columns[now][c]
+
+            def entry(r, c):
+                return jnp.broadcast_to(spread[now % 2, c, r : r + 1, :], (8, 128))
+
             lower = {}
             scale = []
             for c in range(8):
-                value = columns[now][c][c : c + 1]
+                value = entry(c, c)
                 for k in range(c):
                     value = value - lower[c, k] * lower[c, k]
                 scale.append(lax.rsqrt(value))
                 for r in range(c + 1, 8):
-                    value = columns[now][c][r : r + 1]
+                    value = entry(r, c)
                     for k in range(c):
                         value = value - lower[r, k] * lower[c, k]
                     lower[r, c] = value * scale[c]
@@ -434,8 +486,8 @@
                 lines.append(line_now * scale[c])
                 lines_inverse.append(line_inverse * scale[c])
                 at = 8 * now + c
-                pivots[index, at : at + 1, :] = lines[c]
-                solver[index, at : at + 1, :] = lines_inverse[c]
+                pivots[index, at : at + 1, :] = lines[c][0:1]
+                solver[index, at : at + 1, :] = lines_inverse[c][0:1]
             for n in range(now + 1, 8):
                 factors = []
                 for c in range(8):
@@ -472,7 +524,7 @@
         result(index, 0).start()
         result(index, 1).start()
         coupled = solver[index, :, 0:K]
-        return chain[following][:, 0:K] - dot_tn(coupled, coupled, HI)
+        return chain[following][:, 0:K] - triple(dot_tn, coupled, coupled)
 
     lane = iota((K, 8 * K), 1) >> 6
 
@@ -484,13 +536,20 @@
         other = jnp.where(lane == index, other, 0.0)
         return jnp.concatenate([first, other], axis=1)
 
+    own_slot = jnp.where(third, SUB, 0) + sub
+    own_tile = pl.ds(pl.multiple_of((own_slot // 2) * 128, 128), 128)
+
     def solve(index, carry):
         result(index, 0).wait_recv()
         values = solver[index]
-        solved = dot_nn(values[:, K : 2 * K], xin[...], HI)
+        solved = triple(dot_nn, values[:, K : 2 * K], xin[...])
         xall[pl.ds(pl.multiple_of(index * K, K), K), :] = solved
-        following = placed(jnp.minimum(index + 1, SUB - 1))
-        xin[...] = following - dot_tn(values[:, 0:K], solved, HI)
+
+        @pl.when(index < SUB - 1)
+        def _():
+            following = placed(jnp.minimum(index + 1, SUB - 1))
+            xin[...] = following - triple(dot_tn, values[:, 0:K], solved)
+
         return carry
 
     @pl.when(head)
@@ -525,11 +584,12 @@
             arrive(border, border_recv_sem, slot)
         xin[...] = placed(0)
         lax.fori_loop(0, SUB, solve, 0)
-        which = jnp.where(third, SUB, 0) + sub
-        mine = xall[:, pl.ds(pl.multiple_of((which // 2) * 128, 128), 128)]
-        mine = jnp.where(lax.rem(sub, 2) == 1, pltpu.roll(mine, K, 1), mine)
-        factor_out[...] = mine.T[0:K, :]
-        product_out[...] = dot_tn(mine, xall[...], HI)[0:K]
+        odd = lax.rem(sub, 2) == 1
+        mine = xall[:, own_tile]
+        turned = mine.T
+        factor_out[...] = jnp.where(odd, turned[K:], turned[0:K])
+        product = triple(dot_tn, mine, xall[...])
+        product_out[...] = jnp.where(odd, product[K:], product[0:K])
         for step in range(1, SUB):
             line(border, border_send_sem, border_recv_sem, step).wait_send()
 
@@ -660,6 +720,7 @@
             pltpu.VMEM((SUB, K, 2 * K), F32),
             pltpu.VMEM((SUB, K, 128), F32),
             pltpu.VMEM((SUB, K, 2 * K), F32),
+            pltpu.VMEM((2, 8, 8, 128), F32),
             pltpu.VMEM((K, 16 * K), F32),
             pltpu.VMEM((SUB * K, 16 * K), F32),
             pltpu.SemaphoreType.DMA((CX,)),

time: 62.8 us -> 58.4 us (0.930)
  Pallas kernels: 62 us -> 57.4 us
    pallas_call x1, Pallas kernels: 59.3 us -> 54.7 us  [shards(): pl.pallas_call(assemble_kernel, out_shape=(jax.ShapeDtypeStruct((K, 8 * K...]
where the time goes in v1:
time: 58.4 us; the launch traced here: 58.2 us
  Pallas kernels  57.4 us (98%)
  between operations  0.82 us (1%)
    pallas_call x1, Pallas kernels, shards(): pl.pallas_call(assemble_kernel, out_shape=(jax.ShapeDtypeStruct((K, 8 * K...  54.7 us
    pallas_call x1, Pallas kernels, shards(): pl.pallas_call(place_kernel, out_shape=jax.ShapeDtypeStruct((K, 128 * K),...  2.69 us

profile of v1, /device:TPU:2, one launch (start us, length us, event | category | flops | bytes accessed | tf_op | source)
XLA Modules:
  0.0 58.2 jit_solution(4691038826737710664)
XLA Ops:
  0.7 54.7 %assemble.1 = (f32[64,512]{1,0:T(8,128)}, f32[64,512]{1,0:T(8,128)}, f32[64,1024]{1,0:T(8,128)}) custom-call(bf16[64,8,64,256]{3,2,1,0:T(8,128)(2,1)} %defl.1, f32[8,64,256]{2,1,0:T(8,128)} %react.1, s32[1]{0:T(128)S(6)} %copy.4.count), custom_call_target="tpu_custom_call" | custom-call | tf_op jit(solution)/shard_map/assemble/pallas_call | solution.py:688
  55.4 2.7 %place.1 = f32[64,8192]{1,0:T(8,128)} custom-call(f32[64,512]{1,0:T(8,128)} %get-tuple-element.8.own_hbm, f32[64,512]{1,0:T(8,128)} %get-tuple-element.9.factors_hbm, f32[64,1024]{1,0:T(8,128)} %get-tuple-element.10.product_hbm), custom_call_target="tpu_custom_call" | custom-call | tf_op jit(solution)/shard_map/place/pallas_call | solution.py:750

commit v2 on v1

--- a/solution.py
+++ b/solution.py
@@ -57,7 +57,10 @@
     same = (iota(product.shape, 0) & 7) == (iota(product.shape, 1) & 7)
     kept = jnp.where(same, product, 0.0).reshape(K, 8, ROWS).sum(axis=1)
     collect = ((iota((ROWS, K), 0) >> 3) == iota((ROWS, K), 1)).astype(F32)
-    return dot_nn(kept, collect, HI)
+    collect = collect.astype(BF16)
+    high, rest = kept.astype(BF16), kept - kept.astype(BF16).astype(F32)
+    middle, low = halves(rest)
+    return dot_nn(high, collect) + (dot_nn(middle, collect) + dot_nn(low, collect))
 
 
 def assemble_kernel(
@@ -92,6 +95,7 @@
     xin,
     xall,
     load_sem,
+    field_sem,
     mask_send_sem,
     mask_recv_sem,
     face_send_sem,
@@ -125,8 +129,11 @@
     loads = [
         pltpu.make_async_copy(defl.at[:, x], mbuf.at[x], load_sem.at[x]) for x in range(CX)
     ]
-    for load in loads:
+    field = pltpu.make_async_copy(react, weight, field_sem)
+    for load in loads[0:2]:
         load.start()
+    field.start()
+    loads[2].start()
 
     barrier = pltpu.get_barrier_semaphore()
     for step in range(1, SUB):
@@ -146,7 +153,6 @@
 
     live = count[0]
     mask_own[...] = (iota((8, 128), 1) < live).astype(F32)
-    weight[...] = 3.0 + 0.5 * react[...]
     mbuf[CX] = jnp.zeros((K, CY, CZ), BF16)
     acc[...] = jnp.zeros_like(acc)
     part_send[...] = jnp.zeros_like(part_send)
@@ -239,6 +245,12 @@
             z_face(x).start()
 
     def silent_plane(x, carry):
+        @pl.when(x + 3 < CX)
+        def _():
+            pltpu.make_async_copy(
+                defl.at[:, x + 3], mbuf.at[x + 3], load_sem.at[x + 3]
+            ).start()
+
         @pl.when(x < EARLY)
         def _():
             pltpu.make_async_copy(
@@ -265,6 +277,8 @@
         start_faces(x)
         return carry
 
+    field.wait()
+    weight[...] = 3.0 + 0.5 * weight[...]
     loads[0].wait()
     lax.fori_loop(0, 1, silent_plane, 0)
     pl.semaphore_wait(barrier, SUB - 1 + 4)
@@ -524,7 +538,7 @@
         result(index, 0).start()
         result(index, 1).start()
         coupled = solver[index, :, 0:K]
-        return chain[following][:, 0:K] - triple(dot_tn, coupled, coupled)
+        return chain[following][:, 0:K] - dot_tn(coupled, coupled, HI)
 
     lane = iota((K, 8 * K), 1) >> 6
 
@@ -694,7 +708,7 @@
         ),
         in_specs=[
             pl.BlockSpec(memory_space=pl.ANY),
-            vmem,
+            pl.BlockSpec(memory_space=pl.ANY),
             pl.BlockSpec(memory_space=pltpu.SMEM),
         ],
         out_specs=(vmem, vmem, vmem),
@@ -724,6 +738,7 @@
             pltpu.VMEM((K, 16 * K), F32),
             pltpu.VMEM((SUB * K, 16 * K), F32),
             pltpu.SemaphoreType.DMA((CX,)),
+            pltpu.SemaphoreType.DMA,
             pltpu.SemaphoreType.DMA((6,)),
             pltpu.SemaphoreType.DMA((6,)),
             pltpu.SemaphoreType.DMA((2,)),

time: 58.4 us -> 58.7 us (level)
  no operation moved by 1% of the time
where the time goes in v2:
time: 58.7 us; the launch traced here: 58.5 us
  Pallas kernels  57.7 us (98%)
  between operations  0.82 us (1%)
    pallas_call x1, Pallas kernels, shards(): pl.pallas_call(assemble_kernel, out_shape=(jax.ShapeDtypeStruct((K, 8 * K...  55 us
    pallas_call x1, Pallas kernels, shards(): pl.pallas_call(place_kernel, out_shape=jax.ShapeDtypeStruct((K, 128 * K),...  2.69 us

profile of v2, /device:TPU:2, one launch (start us, length us, event | category | flops | bytes accessed | tf_op | source)
XLA Modules:
  0.0 58.5 jit_solution(4880795117465695412)
XLA Ops:
  0.7 55.0 %assemble.1 = (f32[64,512]{1,0:T(8,128)}, f32[64,512]{1,0:T(8,128)}, f32[64,1024]{1,0:T(8,128)}) custom-call(bf16[64,8,64,256]{3,2,1,0:T(8,128)(2,1)} %defl.1, f32[8,64,256]{2,1,0:T(8,128)} %react.1, s32[1]{0:T(128)S(6)} %copy.4.count), custom_call_target="tpu_custom_call" | custom-call | tf_op jit(solution)/shard_map/assemble/pallas_call | solution.py:702
  55.7 2.7 %place.1 = f32[64,8192]{1,0:T(8,128)} custom-call(f32[64,512]{1,0:T(8,128)} %get-tuple-element.8.own_hbm, f32[64,512]{1,0:T(8,128)} %get-tuple-element.9.factors_hbm, f32[64,1024]{1,0:T(8,128)} %get-tuple-element.10.product_hbm), custom_call_target="tpu_custom_call" | custom-call | tf_op jit(solution)/shard_map/place/pallas_call | solution.py:765

commit v3 on v2

--- a/solution.py
+++ b/solution.py
@@ -257,14 +257,8 @@
                 defl.at[:, x + 1], mbuf.at[x + 1], load_sem.at[x + 1]
             ).wait()
 
-        def part(step, inner):
-            for q in range(K // 2 // group):
-                first = pl.multiple_of(step * (K // 2) + q * group, group)
-                row = pl.multiple_of(step * (K // 2 * 8) + q * group * 8, group * 8)
-                stage_group(x, first, row)
-            return inner
-
-        lax.fori_loop(0, 2, part, 0)
+        for first in range(0, K, group):
+            stage_group(x, first, 8 * first)
         ylow[x] = yedge[0].astype(BF16)
         yhigh[x] = yedge[1].astype(BF16)
         product = dot_nt(left[...], right[...])

time: 58.7 us -> 55.7 us (0.949)
  Pallas kernels: 57.7 us -> 54.8 us
    pallas_call x1, Pallas kernels: 55 us -> 52.1 us  [shards(): pl.pallas_call(assemble_kernel, out_shape=(jax.ShapeDtypeStruct((K, 8 * K...]
where the time goes in v3:
time: 55.7 us; the launch traced here: 55.6 us
  Pallas kernels  54.8 us (98%)
  between operations  0.82 us (1%)
    pallas_call x1, Pallas kernels, shards(): pl.pallas_call(assemble_kernel, out_shape=(jax.ShapeDtypeStruct((K, 8 * K...  52.1 us
    pallas_call x1, Pallas kernels, shards(): pl.pallas_call(place_kernel, out_shape=jax.ShapeDtypeStruct((K, 128 * K),...  2.69 us

profile of v3, /device:TPU:2, one launch (start us, length us, event | category | flops | bytes accessed | tf_op | source)
XLA Modules:
  0.0 55.6 jit_solution(9271636699912724987)
XLA Ops:
  0.7 52.1 %assemble.1 = (f32[64,512]{1,0:T(8,128)}, f32[64,512]{1,0:T(8,128)}, f32[64,1024]{1,0:T(8,128)}) custom-call(bf16[64,8,64,256]{3,2,1,0:T(8,128)(2,1)} %defl.1, f32[8,64,256]{2,1,0:T(8,128)} %react.1, s32[1]{0:T(128)S(6)} %copy.4.count), custom_call_target="tpu_custom_call" | custom-call | tf_op jit(solution)/shard_map/assemble/pallas_call | solution.py:696
  52.7 2.7 %place.1 = f32[64,8192]{1,0:T(8,128)} custom-call(f32[64,512]{1,0:T(8,128)} %get-tuple-element.8.own_hbm, f32[64,512]{1,0:T(8,128)} %get-tuple-element.9.factors_hbm, f32[64,1024]{1,0:T(8,128)} %get-tuple-element.10.product_hbm), custom_call_target="tpu_custom_call" | custom-call | tf_op jit(solution)/shard_map/place/pallas_call | solution.py:759
